TPU v7x, 768 devices: a whole 4x8x12 slice. The times are simulated.
768 devices in a mesh: dp: 12 (over z_lo, core), blk: 64 (over y, x, z_hi).
Axes of the slice: x: 4, y: 8, z: 12 (z_hi: 2, z_lo: 6; z = z_hi * 6 + z_lo), core: 2. Of those that a mesh axis runs over, the one named last changes fastest.
Arguments:
- held_acts: bfloat16 [565248, 768], P(('dp', 'blk')), may hold values from -24 to 24
- held_grads: bfloat16 [565248, 1536], P(('dp', 'blk')), may hold values from -6 to 6
- layer_scale: float32 [1536], replicated, may hold values from 0.25 to 4
- out_weight: bfloat16 [768, 1536], P('blk'), may hold values from -0.21875 to 0.21875
- send_slots: int32 [12, 64, 12], P('dp', 'blk'), may hold values from -1 to 22, as said below
- out_source: int32 [12, 64, 12], P('dp', 'blk'), may hold values from 0 to 34, as said below
Outputs:
- grad_acts: bfloat16 [294912, 768], P(('dp', 'blk'))
- grad_weight: float32 [768, 1536], P(('dp', 'blk'))
Inputs may be any that keep to these rules, and one draw needn't show every extreme that they name: `send_slots`: for each device and each dp index e: the held block that the device passes to the device of dp index e with the same blk index, or -1 for none. A device passes nothing to itself, passed blocks are distinct, and none of them is named by the device's own out_source. `out_source`: every block passed by send_slots is named exactly once, by its receiver; no held block is named twice. Each device's blocks below 23 are its blocks 0 to k - 1 for some k, in order, followed by received blocks.
All inputs are finite; a program needn't handle non-finite values.
Results may differ from a plain program's by a relative error of at most 0.0049.
Values may be sent and summed in bfloat16 or wider, within the bound.
A program may use at most 64 MiB of HBM per device.

v0:
```python
import math

import jax
import jax.numpy as jnp
from jax import lax
from jax.sharding import PartitionSpec as P

BLOCK = 32


def project(scaled_rows, out_weight):
    return lax.dot_general(
        scaled_rows,
        lax.all_gather(out_weight, "blk", axis=0, tiled=True),
        (((1,), (1,)), ((), ())),
        preferred_element_type=jnp.float32,
    ).astype(jnp.bfloat16)


def term_maker(act_rows, scaled_rows):
    return lax.dot_general(
        act_rows, scaled_rows, (((0,), (0,)), ((), ())), preferred_element_type=jnp.float32
    )


def on_device(held_acts, held_grads, layer_scale, out_weight, send_slots, out_source):
    n_dp = lax.axis_size("dp")
    n_blk = lax.axis_size("blk")
    inner_width = held_acts.shape[1]
    model_width = held_grads.shape[1]
    out_blocks = out_source.shape[2]
    held_blocks = held_acts.shape[0] // BLOCK
    send_list = send_slots.reshape(n_dp)
    source = out_source.reshape(out_blocks)
    passing = send_list >= 0
    chosen = jnp.maximum(send_list, 0)
    scaled = (layer_scale[None, :] * held_grads.astype(jnp.float32)).astype(jnp.bfloat16)
    act_blocks = held_acts.reshape(held_blocks, BLOCK, inner_width)
    scaled_blocks = scaled.reshape(held_blocks, BLOCK, model_width)
    out_acts = jnp.where(passing[:, None, None], act_blocks[chosen], jnp.zeros((), jnp.bfloat16))
    out_scaled = jnp.where(
        passing[:, None, None], scaled_blocks[chosen], jnp.zeros((), jnp.bfloat16)
    )
    in_acts, in_scaled = (
        lax.all_to_all(out_acts, "dp", split_axis=0, concat_axis=0, tiled=True),
        lax.all_to_all(out_scaled, "dp", split_axis=0, concat_axis=0, tiled=True),
    )
    acts_used = jnp.concatenate([act_blocks, in_acts], 0)[source].reshape(
        out_blocks * BLOCK, inner_width
    )
    scaled_used = jnp.concatenate([scaled_blocks, in_scaled], 0)[source].reshape(
        out_blocks * BLOCK, model_width
    )
    grad_acts = project(scaled_used, out_weight)
    total_rows = n_dp * n_blk * out_blocks * BLOCK
    piece_rows = inner_width // (n_dp * n_blk)
    permuted = (
        acts_used.reshape(-1, n_dp, n_blk, piece_rows)
        .transpose(0, 2, 1, 3)
        .reshape(-1, inner_width)
    )
    partial_sum = lax.psum_scatter(
        term_maker(permuted, scaled_used), "blk", scatter_dimension=0, tiled=True
    )
    summed = lax.psum_scatter(partial_sum, "dp", scatter_dimension=0, tiled=True)
    grad_weight = summed / math.sqrt(total_rows)
    return (grad_acts, grad_weight)


def solution(mesh):
    in_specs = (
        P(("dp", "blk"), None),
        P(("dp", "blk"), None),
        P(),
        P("blk", None),
        P("dp", "blk", None),
        P("dp", "blk", None),
    )
    out_specs = (P(("dp", "blk"), None), P(("dp", "blk"), None))
    return jax.shard_map(
        on_device, mesh=mesh, in_specs=in_specs, out_specs=out_specs, check_vma=False
    )
```

profile of v0, /device:TPU:1, one launch (start us, length us, event | category | flops | bytes accessed | tf_op | source)
XLA Modules:
  0.0 872.3 jit_solution(8031773342338974686)
XLA Ops:
  12.1 14.6 %all-to-all-start.1 = ((bf16[12,32,768]{2,1,0:T(8,128)(2,1)}), bf16[12,32,768]{2,1,0:T(8,128)(2,1)}, u32[]{:S(2)}, u32[]{:S(2)}) async-start(bf16[12,32,768]{2,1,0:T(8,128)(2,1)} %broadcast_select_fusion.1), calls=%async_computation.1 | async-start | bytes 1179648 | tf_op jit(solution)/shard_map/all_to_all | solution.py:45
  30.5 19.0 %all-to-all-done.1 = bf16[12,32,768]{2,1,0:T(8,128)(2,1)} async-done(((bf16[12,32,768]{2,1,0:T(8,128)(2,1)}), bf16[12,32,768]{2,1,0:T(8,128)(2,1)}, u32[]{:S(2)}, u32[]{:S(2)}) %all-to-all-start.1) | async-done | bytes 589856 | tf_op jit(solution)/shard_map/all_to_all | solution.py:45
  49.6 5.9 all-to-all-start
  55.5 2.8 pad_maximum_fusion.1
  58.3 2.9 gather_fusion.3
  61.2 2.9 reshape_reshape.3
  64.0 3.1 copy.9
  69.1 28.5 %all-to-all-done = bf16[12,32,1536]{2,1,0:T(8,128)(2,1)S(1)} async-done(((bf16[12,32,1536]{2,1,0:T(8,128)(2,1)}), bf16[12,32,1536]{2,1,0:T(8,128)(2,1)S(1)}, u32[]{:S(2)}, u32[]{:S(2)}) %all-to-all-start) | async-done | bytes 1179680 | tf_op jit(solution)/shard_map/all_to_all | solution.py:46
  102.3 3.5 fusion.2
  105.8 462.2 %fusion = f32[16,1536]{1,0:T(8,128)S(1)} fusion(f32[768,1536]{1,0:T(8,128)} %fusion.2), kind=kCustom, calls=%all-reduce-scatter | all-reduce-scatter fusion | flops 1572865 | bytes 4820992
  569.4 9.6 %collective-permute-start = (f32[16,1536]{1,0:T(8,128)S(1)}, f32[16,1536]{1,0:T(8,128)S(1)}, u32[]{:S(2)}, u32[]{:S(2)}) collective-permute-start(f32[16,1536]{1,0:T(8,128)S(1)} %fusion), channel_id=1, source_target_pairs={{0,1},{1,2},{2,3},{3,4},{4,5},{5,6},{6,7},{7,8},{8,9},{9,10},{10,1... | collective-permute-start | bytes 294920
  580.3 28.4 %collective-permute-start.10 = (f32[16,1536]{1,0:T(8,128)S(1)}, f32[16,1536]{1,0:T(8,128)S(1)}, u32[]{:S(2)}, u32[]{:S(2)}) collective-permute-start(f32[16,1536]{1,0:T(8,128)S(1)} %fusion), channel_id=1, source_target_pairs={{0,11},{1,12},{2,13},{3,14},{4,15},{5,16},{6,17},{7,18},{8,19},{9,... | collective-permute-start | bytes 294920
  610.0 4.9 collective-permute-start.12
  616.6 3.6 collective-permute-start.14
  620.2 7.4 collective-permute-start.2
  629.8 4.1 collective-permute-start.4
  633.9 4.5 collective-permute-start.5
  638.5 5.0 collective-permute-start.6
  643.5 3.4 collective-permute-start.7
  647.0 4.5 collective-permute-start.8
  656.8 10.8 %concatenate.8 = f32[268,1536]{1,0:T(8,128)S(1)} concatenate(f32[12,1536]{1,0:T(8,128)S(1)} %collective-permute-done.15, f32[16,1536]{1,0:T(8,128)} %copy-done.2, f32[16,1536]{1,0:T(8,128)} %copy-done.1, f32[16,1536]{1,0:T(8,128)S(1)} %collective-permute-done.12, f32[16,1536]{1,0:T(8,128)S(1)} %collective-permute-done.11, f32[16,1536]{1,0:T(8,128)S(1)} %collective-permute-done.10, ...), dimensions={0} | concatenate | bytes 3293184
  670.2 181.1 %all-reduce.5.cloned.1.call-done = f32[12,1536]{1,0:T(8,128)} async-done(((f32[12,1536]{1,0:T(8,128)}), f32[12,1536]{1,0:T(8,128)}) %all-reduce.5.cloned.1.call-update) | async-done | bytes 73744
  853.2 6.1 all-gather.3.cloned.1.call-done
  859.3 3.6 reshape.108
  (69 shorter events, 33.3 us)
Async XLA Ops:
  9.3 17.4 %copy-start.10 = (f32[1536]{0:T(1024)S(1)}, f32[1536]{0:T(1024)}, u32[]{:S(2)}) copy-start(f32[1536]{0:T(1024)} %param.8) | copy-start | bytes 18436
  12.1 37.5 %all-to-all-start.1 = ((bf16[12,32,768]{2,1,0:T(8,128)(2,1)}), bf16[12,32,768]{2,1,0:T(8,128)(2,1)}, u32[]{:S(2)}, u32[]{:S(2)}) async-start(bf16[12,32,768]{2,1,0:T(8,128)(2,1)} %broadcast_select_fusion.1), calls=%async_computation.1 | async-start | bytes 1179648 | tf_op jit(solution)/shard_map/all_to_all | solution.py:45
  30.5 24.9 %copy-start.11 = (s32[1,1,12]{2,1,0:T(1,128)S(1)}, s32[1,1,12]{2,1,0:T(1,128)}, u32[]{:S(2)}) copy-start(s32[1,1,12]{2,1,0:T(1,128)} %param.11) | copy-start | bytes 148
  49.6 48.0 %all-to-all-start = ((bf16[12,32,1536]{2,1,0:T(8,128)(2,1)}), bf16[12,32,1536]{2,1,0:T(8,128)(2,1)S(1)}, u32[]{:S(2)}, u32[]{:S(2)}) async-start(bf16[12,32,1536]{2,1,0:T(8,128)(2,1)} %broadcast_select_fusion), calls=%async_computation | async-start | bytes 2359296 | tf_op jit(solution)/shard_map/all_to_all | solution.py:46
  55.4 795.8 %all-reduce.5.cloned.1.call-start = ((), (), s32[]{:S(2)}) async-start(), calls=%async_computation.3 | async-start | bytes 196608
  568.1 41.9 %collective-permute-start.15 = (f32[12,1536]{1,0:T(8,128)S(1)}, f32[12,1536]{1,0:T(8,128)S(1)}, u32[]{:S(2)}, u32[]{:S(2)}) collective-permute-start(f32[12,1536]{1,0:T(8,128)S(1)} %slice.8), channel_id=1, source_target_pairs={{0,16},{1,17},{2,18},{3,19},{4,20},{5,21},{6,22},{7,23},{8,24},{9,... | collective-permute-start | bytes 221192
  569.4 45.5 %collective-permute-start = (f32[16,1536]{1,0:T(8,128)S(1)}, f32[16,1536]{1,0:T(8,128)S(1)}, u32[]{:S(2)}, u32[]{:S(2)}) collective-permute-start(f32[16,1536]{1,0:T(8,128)S(1)} %fusion), channel_id=1, source_target_pairs={{0,1},{1,2},{2,3},{3,4},{4,5},{5,6},{6,7},{7,8},{8,9},{9,10},{10,1... | collective-permute-start | bytes 294920
  579.0 37.6 %collective-permute-start.1 = (f32[16,1536]{1,0:T(8,128)S(1)}, f32[16,1536]{1,0:T(8,128)S(1)}, u32[]{:S(2)}, u32[]{:S(2)}) collective-permute-start(f32[16,1536]{1,0:T(8,128)S(1)} %fusion), channel_id=1, source_target_pairs={{0,2},{1,3},{2,4},{3,5},{4,6},{5,7},{6,8},{7,9},{8,10},{9,11},{10,... | collective-permute-start | bytes 294920
  580.3 39.9 %collective-permute-start.10 = (f32[16,1536]{1,0:T(8,128)S(1)}, f32[16,1536]{1,0:T(8,128)S(1)}, u32[]{:S(2)}, u32[]{:S(2)}) collective-permute-start(f32[16,1536]{1,0:T(8,128)S(1)} %fusion), channel_id=1, source_target_pairs={{0,11},{1,12},{2,13},{3,14},{4,15},{5,16},{6,17},{7,18},{8,19},{9,... | collective-permute-start | bytes 294920
  608.7 18.9 %collective-permute-start.11 = (f32[16,1536]{1,0:T(8,128)S(1)}, f32[16,1536]{1,0:T(8,128)S(1)}, u32[]{:S(2)}, u32[]{:S(2)}) collective-permute-start(f32[16,1536]{1,0:T(8,128)S(1)} %fusion), channel_id=1, source_target_pairs={{0,12},{1,13},{2,14},{3,15},{4,16},{5,17},{6,18},{7,19},{8,20},{9,... | collective-permute-start | bytes 294920
  610.0 19.8 %collective-permute-start.12 = (f32[16,1536]{1,0:T(8,128)S(1)}, f32[16,1536]{1,0:T(8,128)S(1)}, u32[]{:S(2)}, u32[]{:S(2)}) collective-permute-start(f32[16,1536]{1,0:T(8,128)S(1)} %fusion), channel_id=1, source_target_pairs={{0,13},{1,14},{2,15},{3,16},{4,17},{5,18},{6,19},{7,20},{8,21},{9,... | collective-permute-start | bytes 294920
  614.9 19.0 %collective-permute-start.13 = (f32[16,1536]{1,0:T(8,128)S(1)}, f32[16,1536]{1,0:T(8,128)S(1)}, u32[]{:S(2)}, u32[]{:S(2)}) collective-permute-start(f32[16,1536]{1,0:T(8,128)S(1)} %fusion), channel_id=1, source_target_pairs={{0,14},{1,15},{2,16},{3,17},{4,18},{5,19},{6,20},{7,21},{8,22},{9,... | collective-permute-start | bytes 294920
  616.6 21.9 %collective-permute-start.14 = (f32[16,1536]{1,0:T(8,128)S(1)}, f32[16,1536]{1,0:T(8,128)S(1)}, u32[]{:S(2)}, u32[]{:S(2)}) collective-permute-start(f32[16,1536]{1,0:T(8,128)S(1)} %fusion), channel_id=1, source_target_pairs={{0,15},{1,16},{2,17},{3,18},{4,19},{5,20},{6,21},{7,22},{8,23},{9,... | collective-permute-start | bytes 294920
  620.2 23.3 %collective-permute-start.2 = (f32[16,1536]{1,0:T(8,128)S(1)}, f32[16,1536]{1,0:T(8,128)S(1)}, u32[]{:S(2)}, u32[]{:S(2)}) collective-permute-start(f32[16,1536]{1,0:T(8,128)S(1)} %fusion), channel_id=1, source_target_pairs={{0,3},{1,4},{2,5},{3,6},{4,7},{5,8},{6,9},{7,10},{8,11},{9,12},{10... | collective-permute-start | bytes 294920
  627.6 19.4 %collective-permute-start.3 = (f32[16,1536]{1,0:T(8,128)S(1)}, f32[16,1536]{1,0:T(8,128)S(1)}, u32[]{:S(2)}, u32[]{:S(2)}) collective-permute-start(f32[16,1536]{1,0:T(8,128)S(1)} %fusion), channel_id=1, source_target_pairs={{0,4},{1,5},{2,6},{3,7},{4,8},{5,9},{6,10},{7,11},{8,12},{9,13},{1... | collective-permute-start | bytes 294920
  629.8 21.7 %collective-permute-start.4 = (f32[16,1536]{1,0:T(8,128)S(1)}, f32[16,1536]{1,0:T(8,128)S(1)}, u32[]{:S(2)}, u32[]{:S(2)}) collective-permute-start(f32[16,1536]{1,0:T(8,128)S(1)} %fusion), channel_id=1, source_target_pairs={{0,5},{1,6},{2,7},{3,8},{4,9},{5,10},{6,11},{7,12},{8,13},{9,14},{... | collective-permute-start | bytes 294920
  633.9 17.6 %copy-start.1 = (f32[16,1536]{1,0:T(8,128)}, f32[16,1536]{1,0:T(8,128)S(1)}, u32[]{:S(2)}) copy-start(f32[16,1536]{1,0:T(8,128)S(1)} %collective-permute-done.13) | copy-start | bytes 294916
  633.9 21.5 %collective-permute-start.5 = (f32[16,1536]{1,0:T(8,128)S(1)}, f32[16,1536]{1,0:T(8,128)S(1)}, u32[]{:S(2)}, u32[]{:S(2)}) collective-permute-start(f32[16,1536]{1,0:T(8,128)S(1)} %fusion), channel_id=1, source_target_pairs={{0,6},{1,7},{2,8},{3,9},{4,10},{5,11},{6,12},{7,13},{8,14},{9,15},... | collective-permute-start | bytes 294920
  638.5 15.0 %copy-start.2 = (f32[16,1536]{1,0:T(8,128)}, f32[16,1536]{1,0:T(8,128)S(1)}, u32[]{:S(2)}) copy-start(f32[16,1536]{1,0:T(8,128)S(1)} %collective-permute-done.14) | copy-start | bytes 294916
  638.5 16.9 %collective-permute-start.6 = (f32[16,1536]{1,0:T(8,128)S(1)}, f32[16,1536]{1,0:T(8,128)S(1)}, u32[]{:S(2)}, u32[]{:S(2)}) collective-permute-start(f32[16,1536]{1,0:T(8,128)S(1)} %fusion), channel_id=1, source_target_pairs={{0,7},{1,8},{2,9},{3,10},{4,11},{5,12},{6,13},{7,14},{8,15},{9,16}... | collective-permute-start | bytes 294920
  643.5 11.9 %collective-permute-start.7 = (f32[16,1536]{1,0:T(8,128)S(1)}, f32[16,1536]{1,0:T(8,128)S(1)}, u32[]{:S(2)}, u32[]{:S(2)}) collective-permute-start(f32[16,1536]{1,0:T(8,128)S(1)} %fusion), channel_id=1, source_target_pairs={{0,8},{1,9},{2,10},{3,11},{4,12},{5,13},{6,14},{7,15},{8,16},{9,17... | collective-permute-start | bytes 294920
  647.0 8.5 collective-permute-start.8
  651.5 5.2 collective-permute-start.9
  668.3 191.0 %all-gather.3.cloned.1.call-start = ((), (), s32[]{:S(2)}) async-start(), calls=%async_computation.2 | async-start | bytes 3194880 | tf_op jit(solution)/shard_map/all_gather | solution.py:14
  (8 other events, 23.7 us)
Sparse Core Ops, SparseCore 0:
  668.4 182.7 all-reduce.4
Sparse Core Ops, SparseCore 1:
  674.1 185.2 all-gather.2
where the time goes:
time: 878 us; the launch traced here: 872 us
  blocking collectives  462 us (53%)
  waiting for transfers between devices  235 us (27%)
  starting transfers between devices  106 us (12%)
  local copies, waits for them, and re-layouts  34.9 us (4%)
  between operations  16.6 us (2%)
  other arithmetic  12.3 us (1%)
    unnamed x1, blocking collectives  462 us
    unnamed x19, waiting for transfers between devices  182 us
    unnamed x17, starting transfers between devices  85.1 us
    all_to_all x1, waiting for transfers between devices, on_device(): lax.all_to_all(out_scaled, 'dp', split_axis=0, concat_axis=0, tiled=True)  28.5 us
    all_to_all x1, waiting for transfers between devices, on_device(): lax.all_to_all(out_acts, 'dp', split_axis=0, concat_axis=0, tiled=True)  19 us
    unnamed x30, local copies, waits for them, and re-layouts  19 us
  transfers between devices with their start and end apart: 20, of which 4 were waited for; matrix products, arithmetic and copies ran while one was open for 3% of the time, Pallas kernels for 0%

commit v1 on v0

v1 whole, which is shorter than its diff:
```python
import math

import jax
import jax.numpy as jnp
import ml_dtypes
import numpy as np
from jax import lax
from jax.experimental import pallas as pl
from jax.experimental.pallas import tpu as pltpu
from jax.sharding import PartitionSpec as P

MESH = pl.DeviceIdType.MESH
BF16 = jnp.bfloat16
F32 = jnp.float32
BLOCK = 32
NX, NY, NH, NL, NC = 4, 8, 2, 6, 2
NZ = NH * NL
NDP = NL * NC
HELD, OUT = 23, 12
HD, D = 768, 1536
WROWS = 12
TOTAL_ROWS = NDP * NX * NY * NH * OUT * BLOCK
GROUP = HD // NC // NX


def selection(rows, cols, pairs):
    m = np.zeros((rows, cols), np.float32)
    for r, c in pairs:
        m[r, c] = 1.0
    return m.astype(ml_dtypes.bfloat16)


def tables():
    grad_order = [
        (((c * NX + x) * NY + y) * NZ + h * NL + l, (l * NC + c) * 64 + (y * NX + x) * NH + h)
        for c in range(NC) for x in range(NX) for y in range(NY) for h in range(NH) for l in range(NL)
    ]
    weight_rows = [(WROWS * g + i, 16 * g + i) for g in range(NX * NH) for i in range(WROWS)]
    to_y = [((y * 4 + q) * NZ + z, (q * NY + y) * NZ + z) for q in range(4) for y in range(NY) for z in range(NZ)]
    to_z = [(z * 16 + 3 * q + j, (j * 4 + q) * NZ + z) for j in range(3) for q in range(4) for z in range(NZ)]
    return (
        selection(HD, HD, grad_order),
        selection(GROUP, 16 * NX * NH, weight_rows),
        selection(384, 384, to_y),
        selection(NZ * 16, 256, to_z),
    )


def matmul(a, b, dims=((1,), (0,))):
    return lax.dot_general(a, b, (dims, ((), ())), preferred_element_type=F32)


def kernel(
    acts_hbm, grads_hbm, order_hbm, scale_ref, w_ref, send_ref, source_ref, wsel_ref, ysel_ref, zsel_ref,
    ga_ref, gw_ref,
    acts, grads, order, scaled, acts_t, p_own, p_sib, p_rec, wbuf, wfull,
    xa, xd, xb, ra, rd, rb, ysend, yrecv, zsend, zrecv, gall, sbuf, rbuf,
    load_sem, wh_s, wh_r, wx_s, wx_r, ring_s, ring_r, sib_s, sib_r, pc_s, pc_r, x_s, x_r, y_s, y_r, z_s, z_r, e_s, e_r,
):
    dp = lax.axis_index("dp")
    blk = lax.axis_index("blk")
    zl, core = dp // 2, dp % 2
    y, x, zh = blk // 8, (blk // 2) % 4, blk % 2
    z = zh * NL + zl
    s = 1 - 2 * core

    def at_x(v):
        return (dp, y * 8 + v * 2 + zh)

    def at_y(v):
        return (dp, v * 8 + x * 2 + zh)

    def at_z(v):
        return ((v % NL) * 2 + core, y * 8 + x * 2 + v // NL)

    sibling = (dp + s, blk)
    z_pair = (dp, blk + 1 - 2 * zh)

    def remote(src, dst, ss, rs, dev):
        return pltpu.make_async_remote_copy(
            src_ref=src, dst_ref=dst, send_sem=ss, recv_sem=rs, device_id=dev, device_id_type=MESH
        )

    loads = [
        pltpu.make_async_copy(grads_hbm, grads, load_sem.at[0]),
        pltpu.make_async_copy(acts_hbm, acts.at[pl.ds(0, HELD * BLOCK)], load_sem.at[1]),
        pltpu.make_async_copy(order_hbm, order, load_sem.at[2]),
    ]
    for c in loads:
        c.start()

    barrier = pltpu.get_barrier_semaphore()
    peers = [at_x((x + k) % NX) for k in range(1, NX)]
    peers += [at_y((y + k) % NY) for k in range(1, NY)]
    peers += [at_z((z + k) % NZ) for k in range(1, NZ)]
    peers += [((dp + k - core + 1 - core) % NDP, blk) for k in range(0, NDP, 2)]
    for dev in peers:
        pl.semaphore_signal(barrier, inc=1, device_id=dev, device_id_type=MESH)

    half = pl.ds(pl.multiple_of(core * 768, 768), 768)
    mine = w_ref[:, half].astype(F32)
    wbuf[x, zh] = jnp.concatenate([mine, jnp.zeros((16 - WROWS, 768), F32)], 0).astype(BF16)
    acts[pl.ds(HELD * BLOCK, BLOCK), :] = jnp.zeros((BLOCK, HD), BF16)
    scaled[pl.ds(HELD * BLOCK, BLOCK), :] = jnp.zeros((BLOCK, D), BF16)
    rbuf[dp] = jnp.zeros((BLOCK, HD), BF16)

    pl.semaphore_wait(barrier, len(peers))

    wh = remote(wbuf.at[x, zh], wbuf.at[x, zh], wh_s, wh_r, z_pair)
    wh.start()

    kept = jnp.int32(0)
    for o in range(OUT):
        kept = kept + jnp.where(source_ref[o] < HELD, 1, 0)
    loads[0].wait()
    scale = scale_ref[...]

    def scale_block(j, _):
        used = j < kept
        for e in range(NDP):
            used = used | (send_ref[e] == j)
        factor = jnp.where(used, 1.0, 0.0).astype(F32)
        rows = pl.ds(pl.multiple_of(j * BLOCK, BLOCK), BLOCK)
        scaled[rows, :] = (grads[rows, :].astype(F32) * (scale * factor)).astype(BF16)
        return 0

    lax.fori_loop(0, HELD, scale_block, 0)

    remote(wbuf.at[x, 1 - zh], wbuf.at[x, 1 - zh], wh_s, wh_r, z_pair).wait_recv()
    wx = [remote(wbuf.at[x], wbuf.at[x], wx_s.at[k], wx_r.at[k], at_x((x + k) % NX)) for k in range(1, NX)]
    for c in wx:
        c.start()

    loads[1].wait()
    loads[2].wait()

    def transpose_tile(i, _):
        rows = pl.ds(pl.multiple_of(i * 384, 384), 384)
        acts_t[i] = matmul(order[rows, :], acts[...], ((1,), (1,))).astype(BF16)
        return 0

    lax.fori_loop(0, 2, transpose_tile, 0)

    for k in range(1, NX):
        v = (x - k + NX) % NX
        remote(wbuf.at[v], wbuf.at[v], wx_s.at[k], wx_r.at[k], at_x(v)).wait_recv()

    def wchunk(c, v):
        return wfull.at[c, pl.ds(pl.multiple_of(v * GROUP, GROUP), GROUP)]

    wfull[core, pl.ds(pl.multiple_of(y * GROUP, GROUP), GROUP), :] = matmul(
        wsel_ref[...], wbuf[...].reshape(16 * NX * NH, 768)
    ).astype(BF16)

    def hop(way, k):
        sign = s if way == 0 else -s
        v = (y - sign * k + 2 * NY) % NY
        sem = way * 4 + k
        return remote(wchunk(core, v), wchunk(core, v), ring_s.at[sem], ring_r.at[sem], at_y((y + sign + NY) % NY))

    def arrived(way, k):
        sign = s if way == 0 else -s
        v = (y - sign * (k + 1) + 2 * NY) % NY
        sem = way * 4 + k
        remote(wchunk(core, v), wchunk(core, v), ring_s.at[sem], ring_r.at[sem], at_y(v)).wait_recv()
        return v

    def share(v):
        j = (v - y + NY) % NY
        c = remote(wchunk(core, v), wchunk(core, v), sib_s.at[j], sib_r.at[j], sibling)
        c.start()
        return c

    hops = [hop(0, 0), hop(1, 0)]
    for c in hops:
        c.start()
    shares = [share(y)]

    def advance(k):
        for way, steps in ((0, 4), (1, 3)):
            if k < steps:
                v = arrived(way, k)
                if k + 1 < steps:
                    c = hop(way, k + 1)
                    c.start()
                    hops.append(c)
                shares.append(share(v))

    def term_tile(n, _):
        cols = pl.ds(pl.multiple_of(n * 512, 512), 512)
        t = matmul(acts_t[1 - core], scaled[:, cols]).astype(BF16)
        p_sib[:, :, cols] = t.reshape(NX, GROUP, 512)
        return 0

    lax.fori_loop(0, 3, term_tile, 0)
    order_x = [(x + 2) % NX, (x + s + NX) % NX, (x - s + NX) % NX, x]
    pc = [remote(p_sib.at[v], p_rec.at[v], pc_s.at[k], pc_r.at[k], sibling) for k, v in enumerate(order_x)]
    for c in pc:
        c.start()

    def own_tile(n, _):
        cols = pl.ds(pl.multiple_of(n * 512, 512), 512)
        t = matmul(acts_t[core], scaled[:, cols])
        p_own[:, :, cols] = t.reshape(NX, GROUP, 512)
        return 0

    lax.fori_loop(0, 3, own_tile, 0)

    right, left, far = (x + s + NX) % NX, (x - s + NX) % NX, (x + 2) % NX

    def from_sibling(k, v):
        remote(p_sib.at[v], p_rec.at[v], pc_s.at[k], pc_r.at[k], sibling).wait_recv()
        return p_own[v] + p_rec[v].astype(F32)

    advance(0)
    xa[...] = from_sibling(0, far).astype(BF16)
    ca = remote(xa, ra, x_s.at[0], x_r.at[0], at_x(right))
    ca.start()
    xd[...] = from_sibling(1, left).astype(BF16)
    cd = remote(xd, rd, x_s.at[1], x_r.at[1], at_x(left))
    cd.start()
    advance(1)
    to_right = from_sibling(2, right)
    ca.wait_recv()
    xb[...] = (to_right + ra[...].astype(F32)).astype(BF16)
    cb = remote(xb, rb, x_s.at[2], x_r.at[2], at_x(right))
    cb.start()
    advance(2)
    advance(3)

    for j in range(NY):
        v = (y + j) % NY
        remote(wchunk(1 - core, v), wchunk(1 - core, v), sib_s.at[j], sib_r.at[j], sibling).wait_recv()

    def ga_tile(i, _):
        rows = pl.ds(pl.multiple_of(i * 256, 256), 256)
        t = matmul(scaled[rows, pl.ds(0, 768)], wfull[0], ((1,), (1,)))
        t = t + matmul(scaled[rows, pl.ds(768, 768)], wfull[1], ((1,), (1,)))
        gall[pl.ds(pl.multiple_of(i * 8, 8), 8)] = t.astype(BF16).reshape(8, BLOCK, HD)
        return 0

    lax.fori_loop(0, 3, ga_tile, 0)

    ex = []
    for k in range(1, NDP):
        e = (dp + k) % NDP
        sbuf[k] = gall[jnp.maximum(send_ref[e], 0)]
        c = remote(sbuf.at[k], rbuf.at[dp], e_s.at[k], e_r.at[k], (e, blk))
        c.start()
        ex.append(c)

    mine_x = from_sibling(3, x)
    cd.wait_recv()
    cb.wait_recv()
    t = (mine_x + rd[...].astype(F32) + rb[...].astype(F32)).astype(BF16)
    stacked = jnp.concatenate([t[:, 384 * q : 384 * (q + 1)] for q in range(4)], 0)
    ysend[...] = matmul(ysel_ref[...], stacked).astype(BF16).reshape(NY, 48, 384)
    cy = []
    for k in range(1, NY):
        v = (y + k) % NY
        c = remote(ysend.at[v], yrecv.at[k], y_s.at[k], y_r.at[k], at_y(v))
        c.start()
        cy.append(c)
    total = ysend[y].astype(F32)
    for k in range(1, NY):
        cy[k - 1].wait_recv()
        total = total + yrecv[k].astype(F32)

    tz = total.astype(BF16)
    stacked = jnp.concatenate([tz[:, 128 * j : 128 * (j + 1)] for j in range(3)] + [jnp.zeros((112, 128), BF16)], 0)
    zsend[...] = matmul(zsel_ref[...], stacked).astype(BF16).reshape(NZ, 16, 128)
    cz = []
    for k in range(1, NZ):
        v = (z + k) % NZ
        c = remote(zsend.at[v], zrecv.at[k], z_s.at[k], z_r.at[k], at_z(v))
        c.start()
        cz.append(c)
    total = zsend[z].astype(F32)
    for k in range(1, NZ):
        cz[k - 1].wait_recv()
        total = total + zrecv[k].astype(F32)
    total = total / math.sqrt(TOTAL_ROWS)
    for g in range(12):
        gw_ref[:, pl.ds(128 * g, 128)] = total[g : g + 1, :]

    for c in ex:
        c.wait_recv()
    for o in range(OUT):
        v = source_ref[o]
        local = gall[jnp.minimum(v, HELD - 1)]
        got = rbuf[jnp.maximum(v - HELD, 0)]
        ga_ref[pl.ds(o * BLOCK, BLOCK), :] = jnp.where(v < HELD, local, got)

    for c in [wh, *wx, *hops, *shares, *pc, ca, cd, cb, *cy, *cz, *ex]:
        c.wait_send()


def on_device(held_acts, held_grads, layer_scale, out_weight, send_slots, out_source):
    order, wsel, ysel, zsel = (jnp.asarray(t) for t in tables())
    hbm = pl.BlockSpec(memory_space=pl.ANY)
    vmem = pl.BlockSpec(memory_space=pltpu.VMEM)
    smem = pl.BlockSpec(memory_space=pltpu.SMEM)
    dma = pltpu.SemaphoreType.DMA
    grad_acts, grad_weight = pl.pallas_call(
        kernel,
        out_shape=(
            jax.ShapeDtypeStruct((OUT * BLOCK, HD), BF16),
            jax.ShapeDtypeStruct((1, D), F32),
        ),
        in_specs=[hbm, hbm, hbm, vmem, vmem, smem, smem, vmem, vmem, vmem],
        out_specs=(vmem, vmem),
        scratch_shapes=[
            pltpu.VMEM((HD, HD), BF16),
            pltpu.VMEM((HELD * BLOCK, D), BF16),
            pltpu.VMEM((HD, HD), BF16),
            pltpu.VMEM((HD, D), BF16),
            pltpu.VMEM((NC, HD // NC, HD), BF16),
            pltpu.VMEM((NX, GROUP, D), F32),
            pltpu.VMEM((NX, GROUP, D), BF16),
            pltpu.VMEM((NX, GROUP, D), BF16),
            pltpu.VMEM((NX, NH, 16, 768), BF16),
            pltpu.VMEM((2, HD, 768), BF16),
            *[pltpu.VMEM((GROUP, D), BF16)] * 6,
            pltpu.VMEM((NY, 48, 384), BF16),
            pltpu.VMEM((NY, 48, 384), BF16),
            pltpu.VMEM((NZ, 16, 128), BF16),
            pltpu.VMEM((NZ, 16, 128), BF16),
            pltpu.VMEM((HELD + 1, BLOCK, HD), BF16),
            pltpu.VMEM((NDP, BLOCK, HD), BF16),
            pltpu.VMEM((NDP, BLOCK, HD), BF16),
            dma((3,)),
            dma, dma,
            dma((NX,)), dma((NX,)),
            dma((8,)), dma((8,)),
            dma((8,)), dma((8,)),
            dma((4,)), dma((4,)),
            dma((3,)), dma((3,)),
            dma((NY,)), dma((NY,)),
            dma((NZ,)), dma((NZ,)),
            dma((NDP,)), dma((NDP,)),
        ],
        compiler_params=pltpu.CompilerParams(
            collective_id=0, has_side_effects=True, vmem_limit_bytes=48 * 1024 * 1024
        ),
        cost_estimate=pl.CostEstimate(flops=5_000_000_000, bytes_accessed=8_000_000, transcendentals=0),
    )(
        held_acts,
        held_grads,
        order,
        layer_scale.reshape(1, D),
        out_weight,
        send_slots.reshape(NDP),
        out_source.reshape(OUT),
        wsel,
        ysel,
        zsel,
    )
    return grad_acts, grad_weight


def solution(mesh):
    in_specs = (
        P(("dp", "blk"), None),
        P(("dp", "blk"), None),
        P(),
        P("blk", None),
        P("dp", "blk", None),
        P("dp", "blk", None),
    )
    out_specs = (P(("dp", "blk"), None), P(("dp", "blk"), None))
    return jax.shard_map(
        on_device, mesh=mesh, in_specs=in_specs, out_specs=out_specs, check_vma=False
    )
```

time: 878 us -> 92.1 us (0.10)
  blocking collectives: 462 us -> 0 us
  waiting for transfers between devices: 235 us -> 0 us
  starting transfers between devices: 106 us -> 0 us
  Pallas kernels: 0 us -> 80 us
  local copies, waits for them, and re-layouts: 34.9 us -> 11 us
  between operations: 16.6 us -> 0.65 us
  other arithmetic: 12.3 us -> 0 us
    unnamed x1 -> x0, blocking collectives: 462 us -> none
    unnamed x19 -> x0, waiting for transfers between devices: 182 us -> none
    unnamed x17 -> x0, starting transfers between devices: 85.1 us -> none
    pallas_call x0 -> x1, Pallas kernels: none -> 80 us  [on_device(): pl.pallas_call(kernel, out_shape=(jax.ShapeDtypeStruct((OUT * BLOCK, HD),...]
    all_to_all x2 -> x0, waiting for transfers between devices: 47.5 us -> none  [the longest x1 28.5 us: on_device(): lax.all_to_all(out_scaled, 'dp', split_axis=0, concat_axis=0, tiled=True)]
    all_to_all x2 -> x0, starting transfers between devices: 20.5 us -> none  [the longest x1 14.6 us: on_device(): lax.all_to_all(out_acts, 'dp', split_axis=0, concat_axis=0, tiled=True)]
    unnamed x30 -> x20, local copies, waits for them, and re-layouts: 19 us -> 10.3 us
  transfers between devices with their start and end apart: 20 -> 0, of which waited for: 4 -> 0; matrix products, arithmetic and copies ran while one was open for 3% -> 0% of each run, Pallas kernels for 0% -> 0%
where the time goes in v1:
time: 92.1 us; the launch traced here: 91.6 us
  Pallas kernels  80 us (87%)
  local copies, waits for them, and re-layouts  11 us (12%)
    pallas_call x1, Pallas kernels, on_device(): pl.pallas_call(kernel, out_shape=(jax.ShapeDtypeStruct((OUT * BLOCK, HD),...  80 us
    unnamed x20, local copies, waits for them, and re-layouts  10.3 us

profile of v1, /device:TPU:1, one launch (start us, length us, event | category | flops | bytes accessed | tf_op | source)
XLA Modules:
  0.0 91.6 jit_solution(9967065206090995237)
XLA Ops:
  0.6 0.7 reshape.13.scale_ref
  1.3 0.0 copy-start
  1.3 1.6 %copy-done = bf16[736,1536]{1,0:T(8,128)(2,1)S(1)} copy-done((bf16[736,1536]{1,0:T(8,128)(2,1)S(1)}, bf16[736,1536]{1,0:T(8,128)(2,1)}, u32[]{:S(2)}) %copy-start) | copy-done | bytes 2261016
  3.0 0.0 copy-start.1
  3.0 1.3 %copy-done.1 = bf16[736,768]{1,0:T(8,128)(2,1)S(1)} copy-done((bf16[736,768]{1,0:T(8,128)(2,1)S(1)}, bf16[736,768]{1,0:T(8,128)(2,1)}, u32[]{:S(2)}) %copy-start.1) | copy-done | bytes 1130520
  4.2 0.0 copy-start.2
  4.2 0.8 copy-done.2
  5.0 0.0 copy-start.3
  5.0 0.7 copy-done.3
  5.7 0.0 copy-start.4
  5.7 0.7 copy-done.4
  6.3 0.0 copy-start.5
  6.3 1.3 %copy-done.5 = bf16[768,768]{1,0:T(8,128)(2,1)S(1)} copy-done((bf16[768,768]{1,0:T(8,128)(2,1)S(1)}, bf16[768,768]{1,0:T(8,128)(2,1)}, u32[]{:S(2)}) %copy-start.5) | copy-done | bytes 1179672
  7.6 0.0 copy-start.6
  7.6 1.0 %copy-done.6 = bf16[384,384]{1,0:T(8,128)(2,1)S(1)} copy-done((bf16[384,384]{1,0:T(8,128)(2,1)S(1)}, bf16[384,384]{1,0:T(8,128)(2,1)}, u32[]{:S(2)}) %copy-start.6) | copy-done | bytes 294936
  8.6 0.0 copy-start.7
  8.6 0.9 copy-done.7
  9.5 0.0 copy-start.8
  9.5 0.7 copy-done.8
  10.2 80.0 %shard_map.113 = (bf16[384,768]{1,0:T(8,128)(2,1)S(1)}, f32[1,1536]{1,0:T(1,128)S(1)}) custom-call(bf16[736,768]{1,0:T(8,128)(2,1)S(1)} %copy-done.1, bf16[736,1536]{1,0:T(8,128)(2,1)S(1)} %copy-done, bf16[768,768]{1,0:T(8,128)(2,1)S(1)} %copy-done.5, f32[1,1536]{1,0:T(1,128)S(1)} %reshape.13.scale_ref, bf16[12,1536]{1,0:T(8,128)(2,1)S(1)} %copy-done.2, ...), custom_call_target="tpu_custom_call" | custom-call | flops 5000000000 | bytes 8000000 | tf_op jit(solution)/shard_map/pallas_call | solution.py:304
  90.2 0.8 copy.14
  91.0 0.6 copy.15
Async XLA Ops:
  1.3 1.6 %copy-start = (bf16[736,1536]{1,0:T(8,128)(2,1)S(1)}, bf16[736,1536]{1,0:T(8,128)(2,1)}, u32[]{:S(2)}) copy-start(bf16[736,1536]{1,0:T(8,128)(2,1)} %grads_hbm.1) | copy-start | bytes 6782980
  3.0 1.3 %copy-start.1 = (bf16[736,768]{1,0:T(8,128)(2,1)S(1)}, bf16[736,768]{1,0:T(8,128)(2,1)}, u32[]{:S(2)}) copy-start(bf16[736,768]{1,0:T(8,128)(2,1)} %acts_hbm.1) | copy-start | bytes 3391492
  4.2 0.8 copy-start.2
  5.0 0.7 copy-start.3
  5.7 0.7 copy-start.4
  6.3 1.3 %copy-start.5 = (bf16[768,768]{1,0:T(8,128)(2,1)S(1)}, bf16[768,768]{1,0:T(8,128)(2,1)}, u32[]{:S(2)}) copy-start(bf16[768,768]{1,0:T(8,128)(2,1)} %constant.8.clone.order_hbm) | copy-start | bytes 3538948
  7.6 1.0 %copy-start.6 = (bf16[384,384]{1,0:T(8,128)(2,1)S(1)}, bf16[384,384]{1,0:T(8,128)(2,1)}, u32[]{:S(2)}) copy-start(bf16[384,384]{1,0:T(8,128)(2,1)} %constant.10.clone.ysel_ref) | copy-start | bytes 884740
  8.6 0.9 copy-start.7
  9.5 0.7 copy-start.8

commit v2 on v1

--- a/solution.py
+++ b/solution.py
@@ -21,6 +21,10 @@
 WROWS = 12
 TOTAL_ROWS = NDP * NX * NY * NH * OUT * BLOCK
 GROUP = HD // NC // NX
+PIECES = 3
+PIECE = GROUP // PIECES
+EARLY = (6, 5, 7, 4, 8)
+LATE = (3, 9, 2, 10, 1, 11)
 
 
 def selection(rows, cols, pairs):
@@ -54,7 +58,7 @@
     acts_hbm, grads_hbm, order_hbm, scale_ref, w_ref, send_ref, source_ref, wsel_ref, ysel_ref, zsel_ref,
     ga_ref, gw_ref,
     acts, grads, order, scaled, acts_t, p_own, p_sib, p_rec, wbuf, wfull,
-    xa, xd, xb, ra, rd, rb, ysend, yrecv, zsend, zrecv, gall, sbuf, rbuf,
+    xa, xd, xb, ra, rd, rb, ysend, yrecv, zsend, zrecv, gall, sbuf, rbuf, s_early, r_early, s_late,
     load_sem, wh_s, wh_r, wx_s, wx_r, ring_s, ring_r, sib_s, sib_r, pc_s, pc_r, x_s, x_r, y_s, y_r, z_s, z_r, e_s, e_r,
 ):
     dp = lax.axis_index("dp")
@@ -74,7 +78,6 @@
         return ((v % NL) * 2 + core, y * 8 + x * 2 + v // NL)
 
     sibling = (dp + s, blk)
-    z_pair = (dp, blk + 1 - 2 * zh)
 
     def remote(src, dst, ss, rs, dev):
         return pltpu.make_async_remote_copy(
@@ -101,13 +104,22 @@
     mine = w_ref[:, half].astype(F32)
     wbuf[x, zh] = jnp.concatenate([mine, jnp.zeros((16 - WROWS, 768), F32)], 0).astype(BF16)
     acts[pl.ds(HELD * BLOCK, BLOCK), :] = jnp.zeros((BLOCK, HD), BF16)
-    scaled[pl.ds(HELD * BLOCK, BLOCK), :] = jnp.zeros((BLOCK, D), BF16)
+    scaled[HELD] = jnp.zeros((BLOCK, D), BF16)
     rbuf[dp] = jnp.zeros((BLOCK, HD), BF16)
 
     pl.semaphore_wait(barrier, len(peers))
 
-    wh = remote(wbuf.at[x, zh], wbuf.at[x, zh], wh_s, wh_r, z_pair)
-    wh.start()
+    at_end = (zl == 0) | (zl == NL - 1)
+    first = jnp.where(zl == 0, 3, 0)
+    wh = [
+        remote(wbuf.at[x, zh], wbuf.at[x, zh], wh_s.at[i], wh_r, at_z((1 - zh) * NL + first + i))
+        for i in range(3)
+    ]
+
+    @pl.when(at_end)
+    def _():
+        for c in wh:
+            c.start()
 
     kept = jnp.int32(0)
     for o in range(OUT):
@@ -121,12 +133,22 @@
             used = used | (send_ref[e] == j)
         factor = jnp.where(used, 1.0, 0.0).astype(F32)
         rows = pl.ds(pl.multiple_of(j * BLOCK, BLOCK), BLOCK)
-        scaled[rows, :] = (grads[rows, :].astype(F32) * (scale * factor)).astype(BF16)
+        scaled[j] = (grads[rows, :].astype(F32) * (scale * factor)).astype(BF16)
         return 0
 
     lax.fori_loop(0, HELD, scale_block, 0)
 
-    remote(wbuf.at[x, 1 - zh], wbuf.at[x, 1 - zh], wh_s, wh_r, z_pair).wait_recv()
+    def chosen(k):
+        return jnp.maximum(send_ref[(dp + k) % NDP], 0)
+
+    ex = []
+    for i, k in enumerate(EARLY):
+        s_early[i] = scaled[chosen(k)]
+        c = remote(s_early.at[i], r_early.at[i], e_s.at[k], e_r.at[k], ((dp + k) % NDP, blk))
+        c.start()
+        ex.append(c)
+
+    remote(wbuf.at[x, 1 - zh], wbuf.at[x, 1 - zh], wh_s.at[0], wh_r, sibling).wait_recv()
     wx = [remote(wbuf.at[x], wbuf.at[x], wx_s.at[k], wx_r.at[k], at_x((x + k) % NX)) for k in range(1, NX)]
     for c in wx:
         c.start()
@@ -141,55 +163,15 @@
 
     lax.fori_loop(0, 2, transpose_tile, 0)
 
-    for k in range(1, NX):
-        v = (x - k + NX) % NX
-        remote(wbuf.at[v], wbuf.at[v], wx_s.at[k], wx_r.at[k], at_x(v)).wait_recv()
-
-    def wchunk(c, v):
-        return wfull.at[c, pl.ds(pl.multiple_of(v * GROUP, GROUP), GROUP)]
-
-    wfull[core, pl.ds(pl.multiple_of(y * GROUP, GROUP), GROUP), :] = matmul(
-        wsel_ref[...], wbuf[...].reshape(16 * NX * NH, 768)
-    ).astype(BF16)
-
-    def hop(way, k):
-        sign = s if way == 0 else -s
-        v = (y - sign * k + 2 * NY) % NY
-        sem = way * 4 + k
-        return remote(wchunk(core, v), wchunk(core, v), ring_s.at[sem], ring_r.at[sem], at_y((y + sign + NY) % NY))
-
-    def arrived(way, k):
-        sign = s if way == 0 else -s
-        v = (y - sign * (k + 1) + 2 * NY) % NY
-        sem = way * 4 + k
-        remote(wchunk(core, v), wchunk(core, v), ring_s.at[sem], ring_r.at[sem], at_y(v)).wait_recv()
-        return v
-
-    def share(v):
-        j = (v - y + NY) % NY
-        c = remote(wchunk(core, v), wchunk(core, v), sib_s.at[j], sib_r.at[j], sibling)
-        c.start()
-        return c
-
-    hops = [hop(0, 0), hop(1, 0)]
-    for c in hops:
-        c.start()
-    shares = [share(y)]
-
-    def advance(k):
-        for way, steps in ((0, 4), (1, 3)):
-            if k < steps:
-                v = arrived(way, k)
-                if k + 1 < steps:
-                    c = hop(way, k + 1)
-                    c.start()
-                    hops.append(c)
-                shares.append(share(v))
+    def columns(n):
+        return pl.ds(pl.multiple_of(n * 512, 512), 512)
+
+    def rows_of(n):
+        return scaled[:, :, columns(n)].reshape(HD, 512)
 
     def term_tile(n, _):
-        cols = pl.ds(pl.multiple_of(n * 512, 512), 512)
-        t = matmul(acts_t[1 - core], scaled[:, cols]).astype(BF16)
-        p_sib[:, :, cols] = t.reshape(NX, GROUP, 512)
+        t = matmul(acts_t[1 - core], rows_of(n)).astype(BF16)
+        p_sib[:, :, columns(n)] = t.reshape(NX, GROUP, 512)
         return 0
 
     lax.fori_loop(0, 3, term_tile, 0)
@@ -198,10 +180,58 @@
     for c in pc:
         c.start()
 
+    for k in range(1, NX):
+        v = (x - k + NX) % NX
+        remote(wbuf.at[v], wbuf.at[v], wx_s.at[k], wx_r.at[k], at_x(v)).wait_recv()
+
+    def wchunk(c, v):
+        return wfull.at[c, pl.ds(pl.multiple_of(v * GROUP, GROUP), GROUP)]
+
+    def wpiece(v, p):
+        return wfull.at[core, pl.ds(pl.multiple_of(v * GROUP + p * PIECE, PIECE), PIECE)]
+
+    wfull[core, pl.ds(pl.multiple_of(y * GROUP, GROUP), GROUP), :] = matmul(
+        wsel_ref[...], wbuf[...].reshape(16 * NX * NH, 768)
+    ).astype(BF16)
+
+    hops, shares = [], []
+
+    def sign_of(way):
+        return s if way == 0 else -s
+
+    def hop(way, k, p):
+        v = (y - sign_of(way) * k + 2 * NY) % NY
+        sem = (way * 4 + k) * PIECES + p
+        to = at_y((y + sign_of(way) + NY) % NY)
+        c = remote(wpiece(v, p), wpiece(v, p), ring_s.at[sem], ring_r.at[sem], to)
+        c.start()
+        hops.append(c)
+
+    def share(v):
+        j = (v - y + NY) % NY
+        c = remote(wchunk(core, v), wchunk(core, v), sib_s.at[j], sib_r.at[j], sibling)
+        c.start()
+        shares.append(c)
+
+    for p in range(PIECES):
+        hop(0, 0, p)
+        hop(1, 0, p)
+    share(y)
+
+    def advance(k):
+        for p in range(PIECES):
+            for way, steps in ((0, 4), (1, 3)):
+                if k < steps:
+                    v = (y - sign_of(way) * (k + 1) + 2 * NY) % NY
+                    sem = (way * 4 + k) * PIECES + p
+                    remote(wpiece(v, p), wpiece(v, p), ring_s.at[sem], ring_r.at[sem], at_y(v)).wait_recv()
+                    if k + 1 < steps:
+                        hop(way, k + 1, p)
+                    if p == PIECES - 1:
+                        share(v)
+
     def own_tile(n, _):
-        cols = pl.ds(pl.multiple_of(n * 512, 512), 512)
-        t = matmul(acts_t[core], scaled[:, cols])
-        p_own[:, :, cols] = t.reshape(NX, GROUP, 512)
+        p_own[:, :, columns(n)] = matmul(acts_t[core], rows_of(n)).reshape(NX, GROUP, 512)
         return 0
 
     lax.fori_loop(0, 3, own_tile, 0)
@@ -212,13 +242,15 @@
         remote(p_sib.at[v], p_rec.at[v], pc_s.at[k], pc_r.at[k], sibling).wait_recv()
         return p_own[v] + p_rec[v].astype(F32)
 
-    advance(0)
     xa[...] = from_sibling(0, far).astype(BF16)
     ca = remote(xa, ra, x_s.at[0], x_r.at[0], at_x(right))
     ca.start()
     xd[...] = from_sibling(1, left).astype(BF16)
     cd = remote(xd, rd, x_s.at[1], x_r.at[1], at_x(left))
     cd.start()
+    advance(0)
+    for i, k in enumerate(LATE):
+        s_late[i] = scaled[chosen(k)]
     advance(1)
     to_right = from_sibling(2, right)
     ca.wait_recv()
@@ -232,22 +264,23 @@
         v = (y + j) % NY
         remote(wchunk(1 - core, v), wchunk(1 - core, v), sib_s.at[j], sib_r.at[j], sibling).wait_recv()
 
+    def project(rows):
+        t = matmul(rows[:, :768], wfull[0], ((1,), (1,)))
+        t = t + matmul(rows[:, 768:], wfull[1], ((1,), (1,)))
+        return t.astype(BF16)
+
+    sbuf[...] = project(s_late[...].reshape(len(LATE) * BLOCK, D)).reshape(len(LATE), BLOCK, HD)
+    for i, k in enumerate(LATE):
+        c = remote(sbuf.at[i], rbuf.at[dp], e_s.at[k], e_r.at[k], ((dp + k) % NDP, blk))
+        c.start()
+        ex.append(c)
+
     def ga_tile(i, _):
-        rows = pl.ds(pl.multiple_of(i * 256, 256), 256)
-        t = matmul(scaled[rows, pl.ds(0, 768)], wfull[0], ((1,), (1,)))
-        t = t + matmul(scaled[rows, pl.ds(768, 768)], wfull[1], ((1,), (1,)))
-        gall[pl.ds(pl.multiple_of(i * 8, 8), 8)] = t.astype(BF16).reshape(8, BLOCK, HD)
+        blocks = pl.ds(pl.multiple_of(i * 8, 8), 8)
+        gall[blocks] = project(scaled[blocks].reshape(8 * BLOCK, D)).reshape(8, BLOCK, HD)
         return 0
 
     lax.fori_loop(0, 3, ga_tile, 0)
-
-    ex = []
-    for k in range(1, NDP):
-        e = (dp + k) % NDP
-        sbuf[k] = gall[jnp.maximum(send_ref[e], 0)]
-        c = remote(sbuf.at[k], rbuf.at[dp], e_s.at[k], e_r.at[k], (e, blk))
-        c.start()
-        ex.append(c)
 
     mine_x = from_sibling(3, x)
     cd.wait_recv()
@@ -283,7 +316,12 @@
     for g in range(12):
         gw_ref[:, pl.ds(128 * g, 128)] = total[g : g + 1, :]
 
-    for c in ex:
+    for c in ex[: len(EARLY)]:
+        c.wait_recv()
+    got = project(r_early[...].reshape(len(EARLY) * BLOCK, D)).reshape(len(EARLY), BLOCK, HD)
+    for i, k in enumerate(EARLY):
+        rbuf[(dp - k + NDP) % NDP] = got[i]
+    for c in ex[len(EARLY) :]:
         c.wait_recv()
     for o in range(OUT):
         v = source_ref[o]
@@ -291,7 +329,12 @@
         got = rbuf[jnp.maximum(v - HELD, 0)]
         ga_ref[pl.ds(o * BLOCK, BLOCK), :] = jnp.where(v < HELD, local, got)
 
-    for c in [wh, *wx, *hops, *shares, *pc, ca, cd, cb, *cy, *cz, *ex]:
+    @pl.when(at_end)
+    def _():
+        for c in wh:
+            c.wait_send()
+
+    for c in [*wx, *hops, *shares, *pc, ca, cd, cb, *cy, *cz, *ex]:
         c.wait_send()
 
 
@@ -313,7 +356,7 @@
             pltpu.VMEM((HD, HD), BF16),
             pltpu.VMEM((HELD * BLOCK, D), BF16),
             pltpu.VMEM((HD, HD), BF16),
-            pltpu.VMEM((HD, D), BF16),
+            pltpu.VMEM((HELD + 1, BLOCK, D), BF16),
             pltpu.VMEM((NC, HD // NC, HD), BF16),
             pltpu.VMEM((NX, GROUP, D), F32),
             pltpu.VMEM((NX, GROUP, D), BF16),
@@ -326,12 +369,15 @@
             pltpu.VMEM((NZ, 16, 128), BF16),
             pltpu.VMEM((NZ, 16, 128), BF16),
             pltpu.VMEM((HELD + 1, BLOCK, HD), BF16),
+            pltpu.VMEM((len(LATE), BLOCK, HD), BF16),
             pltpu.VMEM((NDP, BLOCK, HD), BF16),
-            pltpu.VMEM((NDP, BLOCK, HD), BF16),
+            pltpu.VMEM((len(EARLY), BLOCK, D), BF16),
+            pltpu.VMEM((len(EARLY), BLOCK, D), BF16),
+            pltpu.VMEM((len(LATE), BLOCK, D), BF16),
             dma((3,)),
-            dma, dma,
+            dma((3,)), dma,
             dma((NX,)), dma((NX,)),
-            dma((8,)), dma((8,)),
+            dma((8 * PIECES,)), dma((8 * PIECES,)),
             dma((8,)), dma((8,)),
             dma((4,)), dma((4,)),
             dma((3,)), dma((3,)),
@@ -340,7 +386,7 @@
             dma((NDP,)), dma((NDP,)),
         ],
         compiler_params=pltpu.CompilerParams(
-            collective_id=0, has_side_effects=True, vmem_limit_bytes=48 * 1024 * 1024
+            collective_id=0, has_side_effects=True, vmem_limit_bytes=62 * 1024 * 1024
         ),
         cost_estimate=pl.CostEstimate(flops=5_000_000_000, bytes_accessed=8_000_000, transcendentals=0),
     )(

time: 92.1 us -> 74.7 us (0.81)
  Pallas kernels: 80 us -> 70 us
  local copies, waits for them, and re-layouts: 11 us -> 3.81 us
    pallas_call x1, Pallas kernels: 80 us -> 70 us  [on_device(): pl.pallas_call(kernel, out_shape=(jax.ShapeDtypeStruct((OUT * BLOCK, HD),...]
    unnamed x20 -> x4, local copies, waits for them, and re-layouts: 10.3 us -> 2.52 us
where the time goes in v2:
time: 74.7 us; the launch traced here: 74.4 us
  Pallas kernels  70 us (94%)
  local copies, waits for them, and re-layouts  3.81 us (5%)
    pallas_call x1, Pallas kernels, on_device(): pl.pallas_call(kernel, out_shape=(jax.ShapeDtypeStruct((OUT * BLOCK, HD),...  70 us
    unnamed x4, local copies, waits for them, and re-layouts  2.52 us

profile of v2, /device:TPU:1, one launch (start us, length us, event | category | flops | bytes accessed | tf_op | source)
XLA Modules:
  0.0 74.4 jit_solution(977907704520830223)
XLA Ops:
  0.6 1.3 %reshape.13.scale_ref = f32[1,1536]{1,0:T(1,128)} reshape(f32[1536]{0:T(1024)} %param.12) | data formatting | bytes 12288 | tf_op jit(solution)/shard_map/reshape | solution.py:396
  1.9 70.0 %shard_map.113 = (bf16[384,768]{1,0:T(8,128)(2,1)}, f32[1,1536]{1,0:T(1,128)}) custom-call(bf16[736,768]{1,0:T(8,128)(2,1)} %acts_hbm.1, bf16[736,1536]{1,0:T(8,128)(2,1)} %grads_hbm.1, bf16[768,768]{1,0:T(8,128)(2,1)} %constant.8.clone.order_hbm, f32[1,1536]{1,0:T(1,128)} %reshape.13.scale_ref, bf16[12,1536]{1,0:T(8,128)(2,1)} %w_ref.1, s32[12]{0:T(128)} %bitcast.2, ...), custom_call_target="tpu_custom_call" | custom-call | flops 5000000000 | bytes 8000000 | tf_op jit(solution)/shard_map/pallas_call | solution.py:347
  71.9 0.0 copy-start
  71.9 1.9 %copy.14 = bf16[384,768]{1,0:T(8,128)(2,1)} copy(bf16[384,768]{1,0:T(8,128)(2,1)} %get-tuple-element.4) | data formatting | bytes 1179648
  73.8 0.0 copy-done
  73.8 0.6 copy.15
Async XLA Ops:
  71.9 1.9 %copy-start = (f32[1,1536]{1,0:T(1,128)S(1)}, f32[1,1536]{1,0:T(1,128)}, u32[]{:S(2)}) copy-start(f32[1,1536]{1,0:T(1,128)} %get-tuple-element.5) | copy-start | bytes 18436

commit v3 on v2

--- a/solution.py
+++ b/solution.py
@@ -23,8 +23,8 @@
 GROUP = HD // NC // NX
 PIECES = 3
 PIECE = GROUP // PIECES
-EARLY = (6, 5, 7, 4, 8)
-LATE = (3, 9, 2, 10, 1, 11)
+EARLY = (6, 5, 7, 4, 8, 3, 9)
+LATE = (2, 10, 1, 11)
 
 
 def selection(rows, cols, pairs):
@@ -121,11 +121,18 @@
         for c in wh:
             c.start()
 
+    def along_x(h, k, v, to):
+        return remote(wbuf.at[v, h], wbuf.at[v, h], wx_s.at[k], wx_r.at[k], to)
+
+    wx = [along_x(zh, k, x, at_x((x + k) % NX)) for k in range(1, NX)]
+    for c in wx:
+        c.start()
+
     kept = jnp.int32(0)
     for o in range(OUT):
         kept = kept + jnp.where(source_ref[o] < HELD, 1, 0)
     loads[0].wait()
-    scale = scale_ref[...]
+    scale = scale_ref[...].reshape(1, D)
 
     def scale_block(j, _):
         used = j < kept
@@ -149,9 +156,10 @@
         ex.append(c)
 
     remote(wbuf.at[x, 1 - zh], wbuf.at[x, 1 - zh], wh_s.at[0], wh_r, sibling).wait_recv()
-    wx = [remote(wbuf.at[x], wbuf.at[x], wx_s.at[k], wx_r.at[k], at_x((x + k) % NX)) for k in range(1, NX)]
-    for c in wx:
-        c.start()
+    for k in range(1, NX):
+        c = along_x(1 - zh, NX + k, x, at_x((x + k) % NX))
+        c.start()
+        wx.append(c)
 
     loads[1].wait()
     loads[2].wait()
@@ -180,9 +188,41 @@
     for c in pc:
         c.start()
 
+    def own_tile(n, _):
+        p_own[:, :, columns(n)] = matmul(acts_t[core], rows_of(n)).reshape(NX, GROUP, 512)
+        return 0
+
+    lax.fori_loop(0, 3, own_tile, 0)
+
+    right, left, far = (x + s + NX) % NX, (x - s + NX) % NX, (x + 2) % NX
+
+    def from_sibling(k, v):
+        remote(p_sib.at[v], p_rec.at[v], pc_s.at[k], pc_r.at[k], sibling).wait_recv()
+
+    def term(v, h):
+        return p_own[v, :, both[h]] + p_rec[v, :, both[h]].astype(F32)
+
+    both = (pl.ds(0, 768), pl.ds(768, 768))
+
+    def along_ring_x(src, dst, k, h, to):
+        c = remote(src.at[h], dst.at[h], x_s.at[2 * k + h], x_r.at[2 * k + h], at_x(to))
+        c.start()
+        return c
+
+    from_sibling(0, far)
+    ca, cd, cb = [], [], []
+    for h in range(2):
+        xa[h] = term(far, h).astype(BF16)
+        ca.append(along_ring_x(xa, ra, 0, h, right))
+    from_sibling(1, left)
+    for h in range(2):
+        xd[h] = term(left, h).astype(BF16)
+        cd.append(along_ring_x(xd, rd, 1, h, left))
+
     for k in range(1, NX):
         v = (x - k + NX) % NX
-        remote(wbuf.at[v], wbuf.at[v], wx_s.at[k], wx_r.at[k], at_x(v)).wait_recv()
+        along_x(zh, k, v, at_x(v)).wait_recv()
+        along_x(1 - zh, NX + k, v, at_x(v)).wait_recv()
 
     def wchunk(c, v):
         return wfull.at[c, pl.ds(pl.multiple_of(v * GROUP, GROUP), GROUP)]
@@ -230,63 +270,26 @@
                     if p == PIECES - 1:
                         share(v)
 
-    def own_tile(n, _):
-        p_own[:, :, columns(n)] = matmul(acts_t[core], rows_of(n)).reshape(NX, GROUP, 512)
-        return 0
-
-    lax.fori_loop(0, 3, own_tile, 0)
-
-    right, left, far = (x + s + NX) % NX, (x - s + NX) % NX, (x + 2) % NX
-
-    def from_sibling(k, v):
-        remote(p_sib.at[v], p_rec.at[v], pc_s.at[k], pc_r.at[k], sibling).wait_recv()
-        return p_own[v] + p_rec[v].astype(F32)
-
-    xa[...] = from_sibling(0, far).astype(BF16)
-    ca = remote(xa, ra, x_s.at[0], x_r.at[0], at_x(right))
-    ca.start()
-    xd[...] = from_sibling(1, left).astype(BF16)
-    cd = remote(xd, rd, x_s.at[1], x_r.at[1], at_x(left))
-    cd.start()
-    advance(0)
     for i, k in enumerate(LATE):
         s_late[i] = scaled[chosen(k)]
+    advance(0)
+    from_sibling(2, right)
+    for h in range(2):
+        to_right = term(right, h)
+        ca[h].wait_recv()
+        xb[h] = (to_right + ra[h].astype(F32)).astype(BF16)
+        cb.append(along_ring_x(xb, rb, 2, h, right))
     advance(1)
-    to_right = from_sibling(2, right)
-    ca.wait_recv()
-    xb[...] = (to_right + ra[...].astype(F32)).astype(BF16)
-    cb = remote(xb, rb, x_s.at[2], x_r.at[2], at_x(right))
-    cb.start()
     advance(2)
-    advance(3)
-
-    for j in range(NY):
-        v = (y + j) % NY
-        remote(wchunk(1 - core, v), wchunk(1 - core, v), sib_s.at[j], sib_r.at[j], sibling).wait_recv()
-
-    def project(rows):
-        t = matmul(rows[:, :768], wfull[0], ((1,), (1,)))
-        t = t + matmul(rows[:, 768:], wfull[1], ((1,), (1,)))
-        return t.astype(BF16)
-
-    sbuf[...] = project(s_late[...].reshape(len(LATE) * BLOCK, D)).reshape(len(LATE), BLOCK, HD)
-    for i, k in enumerate(LATE):
-        c = remote(sbuf.at[i], rbuf.at[dp], e_s.at[k], e_r.at[k], ((dp + k) % NDP, blk))
-        c.start()
-        ex.append(c)
-
-    def ga_tile(i, _):
-        blocks = pl.ds(pl.multiple_of(i * 8, 8), 8)
-        gall[blocks] = project(scaled[blocks].reshape(8 * BLOCK, D)).reshape(8, BLOCK, HD)
-        return 0
-
-    lax.fori_loop(0, 3, ga_tile, 0)
-
-    mine_x = from_sibling(3, x)
-    cd.wait_recv()
-    cb.wait_recv()
-    t = (mine_x + rd[...].astype(F32) + rb[...].astype(F32)).astype(BF16)
-    stacked = jnp.concatenate([t[:, 384 * q : 384 * (q + 1)] for q in range(4)], 0)
+
+    from_sibling(3, x)
+    quarters = []
+    for h in range(2):
+        cd[h].wait_recv()
+        cb[h].wait_recv()
+        t = (term(x, h) + rd[h].astype(F32) + rb[h].astype(F32)).astype(BF16)
+        quarters += [t[:, :384], t[:, 384:]]
+    stacked = jnp.concatenate(quarters, 0)
     ysend[...] = matmul(ysel_ref[...], stacked).astype(BF16).reshape(NY, 48, 384)
     cy = []
     for k in range(1, NY):
@@ -294,6 +297,31 @@
         c = remote(ysend.at[v], yrecv.at[k], y_s.at[k], y_r.at[k], at_y(v))
         c.start()
         cy.append(c)
+
+    advance(3)
+
+    for j in range(NY):
+        v = (y + j) % NY
+        remote(wchunk(1 - core, v), wchunk(1 - core, v), sib_s.at[j], sib_r.at[j], sibling).wait_recv()
+
+    def project(rows):
+        t = matmul(rows[:, :768], wfull[0], ((1,), (1,)))
+        t = t + matmul(rows[:, 768:], wfull[1], ((1,), (1,)))
+        return t.astype(BF16)
+
+    sbuf[...] = project(s_late[...].reshape(len(LATE) * BLOCK, D)).reshape(len(LATE), BLOCK, HD)
+    for i, k in enumerate(LATE):
+        c = remote(sbuf.at[i], rbuf.at[dp], e_s.at[k], e_r.at[k], ((dp + k) % NDP, blk))
+        c.start()
+        ex.append(c)
+
+    def ga_tile(i, _):
+        blocks = pl.ds(pl.multiple_of(i * 8, 8), 8)
+        gall[blocks] = project(scaled[blocks].reshape(8 * BLOCK, D)).reshape(8, BLOCK, HD)
+        return 0
+
+    lax.fori_loop(0, 3, ga_tile, 0)
+
     total = ysend[y].astype(F32)
     for k in range(1, NY):
         cy[k - 1].wait_recv()
@@ -308,19 +336,18 @@
         c = remote(zsend.at[v], zrecv.at[k], z_s.at[k], z_r.at[k], at_z(v))
         c.start()
         cz.append(c)
-    total = zsend[z].astype(F32)
-    for k in range(1, NZ):
-        cz[k - 1].wait_recv()
-        total = total + zrecv[k].astype(F32)
-    total = total / math.sqrt(TOTAL_ROWS)
-    for g in range(12):
-        gw_ref[:, pl.ds(128 * g, 128)] = total[g : g + 1, :]
-
     for c in ex[: len(EARLY)]:
         c.wait_recv()
     got = project(r_early[...].reshape(len(EARLY) * BLOCK, D)).reshape(len(EARLY), BLOCK, HD)
     for i, k in enumerate(EARLY):
         rbuf[(dp - k + NDP) % NDP] = got[i]
+    total = zsend[z].astype(F32)
+    for k in range(1, NZ):
+        cz[k - 1].wait_recv()
+        total = total + zrecv[k].astype(F32)
+    for g in range(12):
+        gw_ref[:, pl.ds(128 * g, 128)] = total[g : g + 1, :]
+
     for c in ex[len(EARLY) :]:
         c.wait_recv()
     for o in range(OUT):
@@ -334,7 +361,7 @@
         for c in wh:
             c.wait_send()
 
-    for c in [*wx, *hops, *shares, *pc, ca, cd, cb, *cy, *cz, *ex]:
+    for c in [*wx, *hops, *shares, *pc, *ca, *cd, *cb, *cy, *cz, *ex]:
         c.wait_send()
 
 
@@ -363,7 +390,7 @@
             pltpu.VMEM((NX, GROUP, D), BF16),
             pltpu.VMEM((NX, NH, 16, 768), BF16),
             pltpu.VMEM((2, HD, 768), BF16),
-            *[pltpu.VMEM((GROUP, D), BF16)] * 6,
+            *[pltpu.VMEM((2, GROUP, 768), BF16)] * 6,
             pltpu.VMEM((NY, 48, 384), BF16),
             pltpu.VMEM((NY, 48, 384), BF16),
             pltpu.VMEM((NZ, 16, 128), BF16),
@@ -376,11 +403,11 @@
             pltpu.VMEM((len(LATE), BLOCK, D), BF16),
             dma((3,)),
             dma((3,)), dma,
-            dma((NX,)), dma((NX,)),
+            dma((2 * NX,)), dma((2 * NX,)),
             dma((8 * PIECES,)), dma((8 * PIECES,)),
             dma((8,)), dma((8,)),
             dma((4,)), dma((4,)),
-            dma((3,)), dma((3,)),
+            dma((6,)), dma((6,)),
             dma((NY,)), dma((NY,)),
             dma((NZ,)), dma((NZ,)),
             dma((NDP,)), dma((NDP,)),
@@ -393,7 +420,7 @@
         held_acts,
         held_grads,
         order,
-        layer_scale.reshape(1, D),
+        layer_scale,
         out_weight,
         send_slots.reshape(NDP),
         out_source.reshape(OUT),
@@ -401,7 +428,7 @@
         ysel,
         zsel,
     )
-    return grad_acts, grad_weight
+    return grad_acts, grad_weight / math.sqrt(TOTAL_ROWS)
 
 
 def solution(mesh):

time: 74.7 us -> 65.1 us (0.87)
  Pallas kernels: 70 us -> 61 us
  local copies, waits for them, and re-layouts: 3.81 us -> 1.92 us
  other arithmetic: 0 us -> 1.29 us
    pallas_call x1, Pallas kernels: 70 us -> 61 us  [on_device(): pl.pallas_call(kernel, out_shape=(jax.ShapeDtypeStruct((OUT * BLOCK, HD),...]
    reshape x1 -> x0, local copies, waits for them, and re-layouts: 1.3 us -> none  [on_device(): layer_scale.reshape(1, D)]
    div x0 -> x1, other arithmetic: none -> 1.29 us  [on_device(): return (grad_acts, grad_weight / math.sqrt(TOTAL_ROWS))]
    unnamed x4 -> x1, local copies, waits for them, and re-layouts: 2.52 us -> 1.92 us
where the time goes in v3:
time: 65.1 us; the launch traced here: 64.9 us
  Pallas kernels  61 us (94%)
  local copies, waits for them, and re-layouts  1.92 us (3%)
  other arithmetic  1.29 us (2%)
    pallas_call x1, Pallas kernels, on_device(): pl.pallas_call(kernel, out_shape=(jax.ShapeDtypeStruct((OUT * BLOCK, HD),...  61 us
    unnamed x1, local copies, waits for them, and re-layouts  1.92 us

profile of v3, /device:TPU:1, one launch (start us, length us, event | category | flops | bytes accessed | tf_op | source)
XLA Modules:
  0.0 64.9 jit_solution(3355994042867039539)
XLA Ops:
  0.6 61.0 %shard_map.113 = (bf16[384,768]{1,0:T(8,128)(2,1)}, f32[1,1536]{1,0:T(1,128)}) custom-call(bf16[736,768]{1,0:T(8,128)(2,1)} %acts_hbm.1, bf16[736,1536]{1,0:T(8,128)(2,1)} %grads_hbm.1, bf16[768,768]{1,0:T(8,128)(2,1)} %constant.11.clone.order_hbm, f32[1536]{0:T(1024)} %scale_ref.1, bf16[12,1536]{1,0:T(8,128)(2,1)} %w_ref.1, s32[12]{0:T(128)} %bitcast.2, ...), custom_call_target="tpu_custom_call" | custom-call | flops 5000000000 | bytes 8000000 | tf_op jit(solution)/shard_map/pallas_call | solution.py:374
  61.7 1.3 %broadcast_multiply_fusion = f32[1,1536]{1,0:T(1,128)} fusion(f32[1,1536]{1,0:T(1,128)} %get-tuple-element.5), kind=kLoop, calls=%fused_computation | loop fusion | flops 1536 | bytes 12288 | tf_op jit(solution)/shard_map/div | solution.py:431
  63.0 1.9 %copy.13 = bf16[384,768]{1,0:T(8,128)(2,1)} copy(bf16[384,768]{1,0:T(8,128)(2,1)} %get-tuple-element.8) | data formatting | bytes 1179648

commit v4 on v3

--- a/solution.py
+++ b/solution.py
@@ -315,12 +315,6 @@
         c.start()
         ex.append(c)
 
-    def ga_tile(i, _):
-        blocks = pl.ds(pl.multiple_of(i * 8, 8), 8)
-        gall[blocks] = project(scaled[blocks].reshape(8 * BLOCK, D)).reshape(8, BLOCK, HD)
-        return 0
-
-    lax.fori_loop(0, 3, ga_tile, 0)
 
     total = ysend[y].astype(F32)
     for k in range(1, NY):
@@ -336,6 +330,13 @@
         c = remote(zsend.at[v], zrecv.at[k], z_s.at[k], z_r.at[k], at_z(v))
         c.start()
         cz.append(c)
+    def ga_tile(i, _):
+        blocks = pl.ds(pl.multiple_of(i * 8, 8), 8)
+        gall[blocks] = project(scaled[blocks].reshape(8 * BLOCK, D)).reshape(8, BLOCK, HD)
+        return 0
+
+    lax.fori_loop(0, 3, ga_tile, 0)
+
     for c in ex[: len(EARLY)]:
         c.wait_recv()
     got = project(r_early[...].reshape(len(EARLY) * BLOCK, D)).reshape(len(EARLY), BLOCK, HD)

time: 65.1 us -> 65.4 us (level)
  no operation moved by 1% of the time
where the time goes in v4:
time: 65.4 us; the launch traced here: 65.2 us
  Pallas kernels  61.3 us (94%)
  local copies, waits for them, and re-layouts  1.92 us (3%)
  other arithmetic  1.29 us (2%)
    pallas_call x1, Pallas kernels, on_device(): pl.pallas_call(kernel, out_shape=(jax.ShapeDtypeStruct((OUT * BLOCK, HD),...  61.3 us
    unnamed x1, local copies, waits for them, and re-layouts  1.92 us

profile of v4, /device:TPU:1, one launch (start us, length us, event | category | flops | bytes accessed | tf_op | source)
XLA Modules:
  0.0 65.2 jit_solution(649871713727838372)
XLA Ops:
  0.6 61.3 %shard_map.113 = (bf16[384,768]{1,0:T(8,128)(2,1)}, f32[1,1536]{1,0:T(1,128)}) custom-call(bf16[736,768]{1,0:T(8,128)(2,1)} %acts_hbm.1, bf16[736,1536]{1,0:T(8,128)(2,1)} %grads_hbm.1, bf16[768,768]{1,0:T(8,128)(2,1)} %constant.11.clone.order_hbm, f32[1536]{0:T(1024)} %scale_ref.1, bf16[12,1536]{1,0:T(8,128)(2,1)} %w_ref.1, s32[12]{0:T(128)} %bitcast.2, ...), custom_call_target="tpu_custom_call" | custom-call | flops 5000000000 | bytes 8000000 | tf_op jit(solution)/shard_map/pallas_call | solution.py:375
  62.0 1.3 %broadcast_multiply_fusion = f32[1,1536]{1,0:T(1,128)} fusion(f32[1,1536]{1,0:T(1,128)} %get-tuple-element.5), kind=kLoop, calls=%fused_computation | loop fusion | flops 1536 | bytes 12288 | tf_op jit(solution)/shard_map/div | solution.py:432
  63.2 1.9 %copy.13 = bf16[384,768]{1,0:T(8,128)(2,1)} copy(bf16[384,768]{1,0:T(8,128)(2,1)} %get-tuple-element.8) | data formatting | bytes 1179648
